TPU v7x, 32 devices: a whole 2x2x4 slice. The times are simulated.
32 devices in a mesh: groups: 2 (over y), seq: 4 (over z), dp: 4 (over x, core).
Axes of the slice: x: 2, y: 2, z: 4, core: 2. Of those that a mesh axis runs over, the one named last changes fastest.
Arguments:
- inputs: bfloat16 [8, 65536, 512], P(('groups', 'dp'), 'seq'), parts along dimension 0, may hold values from -6 to 6
- cotangent: bfloat16 [8, 65536, 512], P(('groups', 'dp'), 'seq'), parts along dimension 0, may hold values from -6 to 6
- first_factor: bfloat16 [256, 256, 256], P('seq', 'dp'), may hold values from -0.375 to 0.375
- second_factor: bfloat16 [256, 256, 256], P('seq', 'dp'), may hold values from -0.375 to 0.375
Outputs:
- mixed_out: bfloat16 [8, 65536, 512], P(('groups', 'dp'), 'seq'), parts along dimension 0
- input_grad: bfloat16 [8, 65536, 512], P(('groups', 'dp'), 'seq'), parts along dimension 0
- first_factor_grad: bfloat16 [512, 256, 256], P(('groups', 'seq'), 'dp'), parts along dimension 0
- second_factor_grad: bfloat16 [512, 256, 256], P(('groups', 'seq'), 'dp'), parts along dimension 0
There are 2 independent parts, one for each index of `groups`. A program takes and returns all parts, laid end to end along the dimension named above; an argument that names none is the same for every part. Nothing has to cross between parts.
All inputs are finite; a program needn't handle non-finite values.
Results may differ from a plain program's by a relative error of at most 0.009.
Values may be sent and summed in bfloat16 or wider, within the bound.
A program may use at most 320 MiB of HBM per device.

v0:
```python
import math
import jax
import jax.numpy as jnp
from jax import lax
from jax.experimental.layout import Layout, with_layout_constraint
from jax.sharding import PartitionSpec as P


def silu_parts(values):
    sig = jax.nn.sigmoid(values)
    return (values * sig, sig * (1.0 + values * (1.0 - sig)))


def row_major(value):
    return with_layout_constraint(value, Layout(tuple(range(value.ndim))))


def scatter_rows(parts):
    blocks, ring, rows, columns = parts.shape
    flat = parts.reshape(blocks, ring * rows, columns)
    kept = lax.psum_scatter(flat, "dp", scatter_dimension=1, tiled=True)
    return kept.reshape(blocks, kept.shape[1] // rows, rows, columns)


def shards(inputs, cotangent, first_factor, second_factor):
    f32, bf16 = (jnp.float32, jnp.bfloat16)
    seqs = inputs.shape[0]
    rows = inputs.shape[1]
    channels = inputs.shape[2]
    ring = lax.axis_size("seq")
    blocks = first_factor.shape[0]
    columns = second_factor.shape[0]
    width = first_factor.shape[2]
    width_two = second_factor.shape[2]
    norm_scale = 1.0 / math.sqrt(lax.axis_size("dp") * seqs * channels)
    chunks = math.gcd(4, math.gcd(blocks, columns))
    ic, jc = (blocks // chunks, columns // chunks)
    blocked = inputs.reshape(seqs, blocks, width, channels)
    cot_f32 = cotangent.astype(f32)
    gate_value, gate_slope = silu_parts(inputs.astype(f32))

    def after(value, *others):
        kept = lax.optimization_barrier((value,) + others)
        return (kept[0], kept[1:])

    def exchange(part):
        return lax.all_to_all(part, "seq", split_axis=0, concat_axis=0, tiled=True)

    first_parts, received = ([], [])
    for q in range(chunks):
        own = slice(q * ic, (q + 1) * ic)
        factor = lax.all_gather(first_factor[own], "dp", axis=1, tiled=True)
        first_parts.append(factor)
        part = jnp.einsum(
            "ijk,bikc->bijc", factor, blocked[:, own], preferred_element_type=f32
        ).astype(bf16)
        part = part.reshape(seqs, ic, ring, columns, channels).transpose(2, 0, 1, 3, 4)
        part = row_major(part)
        if q:
            part, (received[-1],) = after(part, received[-1])
        received.append(exchange(part))
    second_full = lax.all_gather(second_factor, "dp", axis=1, tiled=True)
    gated_cot = (cot_f32 * gate_value).astype(bf16).reshape(seqs, columns, width_two, channels)
    previous = received
    returned = []
    first_full = jnp.concatenate(first_parts, axis=0)
    first_split = first_full.reshape(blocks, ring, chunks, jc, width)

    def through_first(q, total):
        back = returned[q]
        grad_one = norm_scale * jnp.einsum(
            "sbitc,bikc->istk", back, blocked, preferred_element_type=f32
        )
        total = total + jnp.einsum(
            "istk,sbitc->bikc", first_split[:, :, q], back, preferred_element_type=f32
        )
        return (grad_one.astype(bf16), total)

    grads_one = []
    done = 0
    for q in range(chunks):
        own = slice(q * jc, (q + 1) * jc)
        part = jnp.einsum(
            "jik,bjic->bkjc", second_full[own], gated_cot[:, own], preferred_element_type=f32
        ).astype(bf16)
        part = part.reshape(seqs, ring, blocks, jc, channels).transpose(1, 0, 2, 3, 4)
        part = row_major(part)
        if q == chunks // 2:
            exchanged = jnp.concatenate(received, axis=2).transpose(1, 0, 2, 3, 4)
            exchanged = exchanged.reshape(seqs, ring * blocks, columns, channels)
            mixing = jnp.einsum(
                "jik,bkjc->bjic", second_full, exchanged, preferred_element_type=f32
            ).reshape(seqs, rows, channels)
            outputs = (mixing * gate_value).astype(bf16)
            grad_two = norm_scale * jnp.einsum(
                "bjic,bkjc->jik", gated_cot, exchanged, preferred_element_type=f32
            )
            grad_two = grad_two.astype(bf16)
            total = (cot_f32 * mixing * gate_slope).reshape(blocked.shape)
            part, (outputs, grad_two, total) = after(part, outputs, grad_two, total)
            second_sum = lax.psum_scatter(grad_two, "dp", scatter_dimension=1, tiled=True)
        elif q > chunks // 2:
            while done < q - 1:
                grad_one, total = through_first(done, total)
                grads_one.append(grad_one)
                done += 1
            part, (total, *grads_one) = after(part, total, *grads_one)
            grads_one = list(grads_one)
        part, (previous[-1],) = after(part, previous[-1])
        returned.append(exchange(part))
        previous = returned
    while done < chunks - 1:
        grad_one, total = through_first(done, total)
        grads_one.append(grad_one)
        done += 1
    first_sums = []
    if grads_one:
        early = jnp.concatenate(grads_one, axis=2)
        early_sum = scatter_rows(early)
        returned[-1], (early_sum, total, second_sum) = after(
            returned[-1], early_sum, total, second_sum
        )
        first_sums.append(early_sum)
    grad_one, total = through_first(chunks - 1, total)
    first_sums.append(scatter_rows(grad_one))
    first_sum = jnp.concatenate(first_sums, axis=2).reshape(first_factor.shape)
    input_grad = total.reshape(seqs, rows, channels).astype(bf16)
    return (outputs, input_grad, first_sum, second_sum)


def solution(mesh):
    in_specs = (
        P(("groups", "dp"), "seq", None),
        P(("groups", "dp"), "seq", None),
        P("seq", "dp", None),
        P("seq", "dp", None),
    )
    out_specs = (
        P(("groups", "dp"), "seq", None),
        P(("groups", "dp"), "seq", None),
        P(("groups", "seq"), "dp", None),
        P(("groups", "seq"), "dp", None),
    )
    return jax.shard_map(shards, mesh=mesh, in_specs=in_specs, out_specs=out_specs, check_vma=False)
```

profile of v0, /device:TPU:0, one launch (start us, length us, event | category | flops | bytes accessed | tf_op | source)
XLA Modules:
  0.0 951.7 jit_solution(6830200255525887186)
XLA Ops:
  10.1 25.4 %all-gather.10.cloned.1.call-done = bf16[16,256,256]{2,1,0:T(8,128)(2,1)} async-done(((bf16[16,64,256]{2,1,0:T(8,128)(2,1)}), bf16[16,256,256]{2,1,0:T(8,128)(2,1)}) %all-gather.10.cloned.1.call-update) | async-done | bytes 2097168 | tf_op jit(solution)/shard_map/all_gather | solution.py:52
  48.3 24.6 %all-gather.8.cloned.1.call-done = bf16[16,256,256]{2,1,0:T(8,128)(2,1)} async-done(((bf16[16,64,256]{2,1,0:T(8,128)(2,1)}), bf16[16,256,256]{2,1,0:T(8,128)(2,1)}) %all-gather.8.cloned.1.call-update) | async-done | bytes 2097168 | tf_op jit(solution)/shard_map/all_gather | solution.py:52
  79.2 61.5 %all-to-all-done = bf16[4,1,16,64,512]{4,3,2,1,0:T(8,128)(2,1)} async-done(((bf16[4,1,16,64,512]{4,3,2,1,0:T(8,128)(2,1)}), bf16[4,1,16,64,512]{4,3,2,1,0:T(8,128)(2,1)}, u32[]{:S(2)}, u32[]{:S(2)}) %all-to-all-start) | async-done | bytes 4194336 | tf_op jit(solution)/shard_map/all_to_all | solution.py:47
  155.2 83.5 %all-to-all-done.1 = bf16[4,1,16,64,512]{4,3,2,1,0:T(8,128)(2,1)} async-done(((bf16[4,1,16,64,512]{4,3,2,1,0:T(8,128)(2,1)}), bf16[4,1,16,64,512]{4,3,2,1,0:T(8,128)(2,1)}, u32[]{:S(2)}, u32[]{:S(2)}) %all-to-all-start.1) | async-done | bytes 4194336 | tf_op jit(solution)/shard_map/all_to_all | solution.py:47
  250.0 86.3 %all-to-all-done.2 = bf16[4,1,16,64,512]{4,3,2,1,0:T(8,128)(2,1)} async-done(((bf16[4,1,16,64,512]{4,3,2,1,0:T(8,128)(2,1)}), bf16[4,1,16,64,512]{4,3,2,1,0:T(8,128)(2,1)}, u32[]{:S(2)}, u32[]{:S(2)}) %all-to-all-start.2) | async-done | bytes 4194336 | tf_op jit(solution)/shard_map/all_to_all | solution.py:47
  341.3 21.3 %fusion = bf16[1,16384,512]{2,1,0:T(8,128)(2,1)} fusion(bf16[1,16384,512]{2,1,0:T(8,128)(2,1)} %param.5, bf16[1,16384,512]{2,1,0:T(8,128)(2,1)} %param.4), kind=kLoop, calls=%fused_computation.5 | loop fusion | flops 67108864 | bytes 50331648 | tf_op jit(solution)/shard_map/convert_element_type | solution.py:63
  388.0 46.1 %all-to-all-done.3 = bf16[4,1,16,64,512]{4,3,2,1,0:T(8,128)(2,1)} async-done(((bf16[4,1,16,64,512]{4,3,2,1,0:T(8,128)(2,1)}), bf16[4,1,16,64,512]{4,3,2,1,0:T(8,128)(2,1)}, u32[]{:S(2)}, u32[]{:S(2)}) %all-to-all-start.3) | async-done | bytes 4194336 | tf_op jit(solution)/shard_map/all_to_all | solution.py:47
  439.3 14.0 %pad_maximum_fusion = bf16[4,1,64,64,512]{4,3,2,1,0:T(8,128)(2,1)} fusion(bf16[4,1,16,64,512]{4,3,2,1,0:T(8,128)(2,1)} %all-to-all-done.3, bf16[4,1,16,64,512]{4,3,2,1,0:T(8,128)(2,1)} %all-to-all-done.2, bf16[4,1,16,64,512]{4,3,2,1,0:T(8,128)(2,1)} %all-to-all-done.1, bf16[4,1,16,64,512]{4,3,2,1,0:T(8,128)(2,1)} %all-to-all-done), kind=kLoop, calls=%fused_computation.19 | loop fusion | flops 25165824 | bytes 33554432 | tf_op jit(solution)/shard_map/concatenate | solution.py:89
  453.3 51.6 %fusion.11 = f32[64,512,256]{1,2,0:T(8,128)} fusion(bf16[256,64,512]{2,1,0:T(8,128)(2,1)} %bitcast.197, bf16[64,256,256]{2,0,1:T(8,128)(2,1)} %all-gather.6.cloned.1.call-done), kind=kOutput, calls=%fused_computation.23 | convolution fusion | flops 4294967296 | bytes 58720256 | tf_op jit(solution)/shard_map/jik,bkjc->bjic/dot_general | solution.py:91
  504.9 40.1 %fusion.1 = (f32[1,16384,512]{2,1,0:T(8,128)}, bf16[1,16384,512]{2,1,0:T(8,128)(2,1)}) fusion(bf16[1,16384,512]{2,1,0:T(8,128)(2,1)} %param.5, bf16[1,16384,512]{2,1,0:T(8,128)(2,1)} %param.4, f32[64,512,256]{1,2,0:T(8,128)} %fusion.11), kind=kLoop, calls=%fused_computation.6 | loop fusion | flops 117440512 | bytes 117440512 | tf_op jit(solution)/shard_map/mul | solution.py:99
  545.0 24.3 %multiply_convert_fusion = bf16[64,256,256]{2,1,0:T(8,128)(2,1)} fusion(bf16[64,256,512]{2,1,0:T(8,128)(2,1)} %bitcast.199, bf16[256,64,512]{2,1,0:T(8,128)(2,1)} %bitcast.198), kind=kOutput, calls=%fused_computation.20 | convolution fusion | flops 4303355904 | bytes 41943040 | tf_op jit(solution)/shard_map/bjic,bkjc->jik/dot_general | solution.py:95
  600.8 33.7 %copy.73 = f32[1,64,256,512]{2,3,1,0:T(8,128)} copy(f32[1,64,256,512]{3,2,1,0:T(8,128)} %bitcast.196) | data formatting | bytes 67108864 | tf_op jit(solution)/shard_map/optimization_barrier | solution.py:43
  634.6 17.9 %fusion.36 = f32[64,512,256,1]{2,1,0,3:T(8,128)} fusion(bf16[64,4,1,16,256]{4,3,2,1,0:T(8,128)(2,1)S(1)} %get-tuple-element.61, bf16[4,1,64,16,512]{4,3,2,1,0:T(8,128)(2,1)} %all-to-all-done.4), kind=kOutput, calls=%fused_computation.73 | convolution fusion | flops 1073741824 | bytes 39845888 | tf_op jit(solution)/shard_map/istk,sbitc->bikc/dot_general | solution.py:74
  652.4 24.2 %all-to-all-done.5 = bf16[4,1,64,16,512]{4,3,2,1,0:T(8,128)(2,1)} async-done(((bf16[4,1,64,16,512]{4,3,2,1,0:T(8,128)(2,1)}), bf16[4,1,64,16,512]{4,3,2,1,0:T(8,128)(2,1)}, u32[]{:S(2)}, u32[]{:S(2)}) %all-to-all-start.5) | async-done | bytes 4194336 | tf_op jit(solution)/shard_map/all_to_all | solution.py:47
  681.6 10.2 %multiply_convert_fusion.4 = bf16[64,4,16,256]{3,2,1,0:T(8,128)(2,1)S(1)} fusion(bf16[64,256,512,1]{2,1,3,0:T(8,128)(2,1)} %bitcast.192, bf16[4,1,64,16,512]{4,3,2,1,0:T(8,128)(2,1)} %all-to-all-done.4), kind=kOutput, calls=%fused_computation.59 | convolution fusion | flops 1075838976 | bytes 23068672 | tf_op jit(solution)/shard_map/sbitc,bikc->istk/dot_general | solution.py:71
  691.8 11.3 %multiply_convert_fusion.3 = bf16[64,4,16,256]{3,2,1,0:T(8,128)(2,1)} fusion(bf16[64,256,512,1]{2,1,3,0:T(8,128)(2,1)} %bitcast.193, bf16[4,1,64,16,512]{4,3,2,1,0:T(8,128)(2,1)} %all-to-all-done.5), kind=kOutput, calls=%fused_computation.58 | convolution fusion | flops 1075838976 | bytes 23068672 | tf_op jit(solution)/shard_map/sbitc,bikc->istk/dot_general | solution.py:71
  703.1 35.8 %bitcast_add_fusion.2 = f32[1,64,256,512]{2,3,1,0:T(8,128)} fusion(f32[1,64,256,512]{2,3,1,0:T(8,128)} %copy.73, f32[64,512,256,1]{2,1,0,3:T(8,128)} %fusion.36, bf16[64,4,1,16,256]{4,3,2,1,0:T(8,128)(2,1)} %get-tuple-element.60, bf16[4,1,64,16,512]{4,3,2,1,0:T(8,128)(2,1)} %all-to-all-done.5), kind=kOutput, calls=%fused_computation.15 | convolution fusion | flops 1090519040 | bytes 106954752 | tf_op jit(solution)/shard_map/istk,sbitc->bikc/dot_general | solution.py:74
  738.9 35.3 %all-to-all-done.6 = bf16[4,1,64,16,512]{4,3,2,1,0:T(8,128)(2,1)} async-done(((bf16[4,1,64,16,512]{4,3,2,1,0:T(8,128)(2,1)}), bf16[4,1,64,16,512]{4,3,2,1,0:T(8,128)(2,1)}, u32[]{:S(2)}, u32[]{:S(2)}) %all-to-all-start.6) | async-done | bytes 4194336 | tf_op jit(solution)/shard_map/all_to_all | solution.py:47
  774.2 10.1 %multiply_convert_fusion.2 = bf16[64,4,16,256]{3,2,1,0:T(8,128)(2,1)S(1)} fusion(bf16[64,256,512,1]{2,1,3,0:T(8,128)(2,1)} %bitcast.194, bf16[4,1,64,16,512]{4,3,2,1,0:T(8,128)(2,1)} %all-to-all-done.6), kind=kOutput, calls=%fused_computation.57 | convolution fusion | flops 1075838976 | bytes 23068672 | tf_op jit(solution)/shard_map/sbitc,bikc->istk/dot_general | solution.py:71
  795.7 25.4 %bitcast_add_fusion.1 = f32[1,64,256,512]{2,3,1,0:T(8,128)} fusion(f32[1,64,256,512]{2,3,1,0:T(8,128)} %bitcast_add_fusion.2, bf16[64,4,1,16,256]{4,3,2,1,0:T(8,128)(2,1)S(1)} %copy-done.2, bf16[4,1,64,16,512]{4,3,2,1,0:T(8,128)(2,1)} %all-to-all-done.6), kind=kOutput, calls=%fused_computation.14 | convolution fusion | flops 1082130432 | bytes 73400320 | tf_op jit(solution)/shard_map/istk,sbitc->bikc/dot_general | solution.py:74
  821.2 67.2 %all-to-all-done.7 = bf16[4,1,64,16,512]{4,3,2,1,0:T(8,128)(2,1)} async-done(((bf16[4,1,64,16,512]{4,3,2,1,0:T(8,128)(2,1)}), bf16[4,1,64,16,512]{4,3,2,1,0:T(8,128)(2,1)}, u32[]{:S(2)}, u32[]{:S(2)}) %all-to-all-start.7) | async-done | bytes 4194336 | tf_op jit(solution)/shard_map/all_to_all | solution.py:47
  888.4 11.5 %multiply_convert_fusion.1 = bf16[64,4,16,256]{3,2,1,0:T(8,128)(2,1)} fusion(bf16[64,256,512,1]{2,1,3,0:T(8,128)(2,1)} %bitcast.195, bf16[4,1,64,16,512]{4,3,2,1,0:T(8,128)(2,1)} %all-to-all-done.7), kind=kOutput, calls=%fused_computation.56 | convolution fusion | flops 1075838976 | bytes 23068672 | tf_op jit(solution)/shard_map/sbitc,bikc->istk/dot_general | solution.py:71
  899.9 19.3 %fusion.7 = bf16[1,64,256,512]{2,3,1,0:T(8,128)(2,1)} fusion(f32[1,64,256,512]{2,3,1,0:T(8,128)} %bitcast_add_fusion.1, bf16[64,4,1,16,256]{4,3,2,1,0:T(8,128)(2,1)S(1)} %copy-done.6, bf16[4,1,64,16,512]{4,3,2,1,0:T(8,128)(2,1)} %all-to-all-done.7), kind=kOutput, calls=%fused_computation.13 | convolution fusion | flops 1090519040 | bytes 56623104 | tf_op jit(solution)/shard_map/istk,sbitc->bikc/dot_general | solution.py:74
  919.2 22.6 %copy.81 = bf16[1,64,256,512]{3,2,1,0:T(8,128)(2,1)} copy(bf16[1,64,256,512]{2,3,1,0:T(8,128)(2,1)} %fusion.7) | data formatting | bytes 33554432 | tf_op jit(solution)/shard_map/convert_element_type | solution.py:127
  (70 shorter events, 133.8 us)
Async XLA Ops:
  7.2 28.4 %all-gather.10.cloned.1.call-start = ((), (), s32[]{:S(2)}) async-start(), calls=%async_computation.13 | async-start | bytes 2621440 | tf_op jit(solution)/shard_map/all_gather | solution.py:52
  41.9 98.8 %all-to-all-start = ((bf16[4,1,16,64,512]{4,3,2,1,0:T(8,128)(2,1)}), bf16[4,1,16,64,512]{4,3,2,1,0:T(8,128)(2,1)}, u32[]{:S(2)}, u32[]{:S(2)}) async-start(bf16[4,1,16,64,512]{4,3,2,1,0:T(8,128)(2,1)} %bitcast.212), calls=%async_computation | async-start | bytes 8388608 | tf_op jit(solution)/shard_map/all_to_all | solution.py:47
  46.8 26.0 %all-gather.8.cloned.1.call-start = ((), (), s32[]{:S(2)}) async-start(), calls=%async_computation.12 | async-start | bytes 2621440 | tf_op jit(solution)/shard_map/all_gather | solution.py:52
  47.6 101.3 %all-gather.12.cloned.1.call-start = ((), (), s32[]{:S(2)}) async-start(), calls=%async_computation.14 | async-start | bytes 2621440 | tf_op jit(solution)/shard_map/all_gather | solution.py:52
  140.7 5.6 copy-start.5
  140.7 98.1 %all-to-all-start.1 = ((bf16[4,1,16,64,512]{4,3,2,1,0:T(8,128)(2,1)}), bf16[4,1,16,64,512]{4,3,2,1,0:T(8,128)(2,1)}, u32[]{:S(2)}, u32[]{:S(2)}) async-start(bf16[4,1,16,64,512]{4,3,2,1,0:T(8,128)(2,1)} %bitcast.211), calls=%async_computation.1 | async-start | bytes 8388608 | tf_op jit(solution)/shard_map/all_to_all | solution.py:47
  145.7 97.9 %all-gather.14.cloned.1.call-start = ((), (), s32[]{:S(2)}) async-start(), calls=%async_computation.15 | async-start | bytes 2621440 | tf_op jit(solution)/shard_map/all_gather | solution.py:52
  146.3 216.3 %all-gather.6.cloned.1.call-start = ((), (), s32[]{:S(2)}) async-start(), calls=%async_computation.11 | async-start | bytes 10485760 | tf_op jit(solution)/shard_map/all_gather | solution.py:62
  238.8 97.5 %all-to-all-start.2 = ((bf16[4,1,16,64,512]{4,3,2,1,0:T(8,128)(2,1)}), bf16[4,1,16,64,512]{4,3,2,1,0:T(8,128)(2,1)}, u32[]{:S(2)}, u32[]{:S(2)}) async-start(bf16[4,1,16,64,512]{4,3,2,1,0:T(8,128)(2,1)} %bitcast.215), calls=%async_computation.2 | async-start | bytes 8388608 | tf_op jit(solution)/shard_map/all_to_all | solution.py:47
  336.3 97.7 %all-to-all-start.3 = ((bf16[4,1,16,64,512]{4,3,2,1,0:T(8,128)(2,1)}), bf16[4,1,16,64,512]{4,3,2,1,0:T(8,128)(2,1)}, u32[]{:S(2)}, u32[]{:S(2)}) async-start(bf16[4,1,16,64,512]{4,3,2,1,0:T(8,128)(2,1)} %bitcast.214), calls=%async_computation.3 | async-start | bytes 8388608 | tf_op jit(solution)/shard_map/all_to_all | solution.py:47
  362.6 9.8 %copy-start = (bf16[1,16384,512]{2,1,0:T(8,128)(2,1)S(1)}, bf16[1,16384,512]{2,1,0:T(8,128)(2,1)}, u32[]{:S(2)}) copy-start(bf16[1,16384,512]{2,1,0:T(8,128)(2,1)} %fusion) | copy-start | bytes 50331652
  434.0 144.8 %all-to-all-start.4 = ((bf16[4,1,64,16,512]{4,3,2,1,0:T(8,128)(2,1)}), bf16[4,1,64,16,512]{4,3,2,1,0:T(8,128)(2,1)}, u32[]{:S(2)}, u32[]{:S(2)}) async-start(bf16[4,1,64,16,512]{4,3,2,1,0:T(8,128)(2,1)} %bitcast.210), calls=%async_computation.4 | async-start | bytes 8388608 | tf_op jit(solution)/shard_map/all_to_all | solution.py:47
  438.9 382.3 %reduce-scatter.6.cloned.1.call-start = ((), (), s32[]{:S(2)}) async-start(), calls=%async_computation.17 | async-start | bytes 10485760 | tf_op jit(solution)/shard_map/reduce_scatter | solution.py:101
  578.9 5.5 copy-start.3
  578.9 97.8 %all-to-all-start.5 = ((bf16[4,1,64,16,512]{4,3,2,1,0:T(8,128)(2,1)}), bf16[4,1,64,16,512]{4,3,2,1,0:T(8,128)(2,1)}, u32[]{:S(2)}, u32[]{:S(2)}) async-start(bf16[4,1,64,16,512]{4,3,2,1,0:T(8,128)(2,1)} %bitcast.213), calls=%async_computation.5 | async-start | bytes 8388608 | tf_op jit(solution)/shard_map/all_to_all | solution.py:47
  588.5 2.9 copy-start.4
  676.7 97.6 %all-to-all-start.6 = ((bf16[4,1,64,16,512]{4,3,2,1,0:T(8,128)(2,1)}), bf16[4,1,64,16,512]{4,3,2,1,0:T(8,128)(2,1)}, u32[]{:S(2)}, u32[]{:S(2)}) async-start(bf16[4,1,64,16,512]{4,3,2,1,0:T(8,128)(2,1)} %bitcast.208), calls=%async_computation.6 | async-start | bytes 8388608 | tf_op jit(solution)/shard_map/all_to_all | solution.py:47
  681.5 206.8 %reduce-scatter.4.cloned.1.call-start = ((), (), s32[]{:S(2)}) async-start(), calls=%async_computation.16 | async-start | bytes 7864320 | tf_op jit(solution)/shard_map/reduce_scatter | solution.py:21
  774.2 10.1 %copy-start.1 = (bf16[64,4,16,256]{3,2,1,0:T(8,128)(2,1)S(1)}, bf16[64,4,16,256]{3,2,1,0:T(8,128)(2,1)}, u32[]{:S(2)}) copy-start(bf16[64,4,16,256]{3,2,1,0:T(8,128)(2,1)} %multiply_convert_fusion.3) | copy-start | bytes 6291460
  790.7 5.1 copy-start.2
  790.7 97.7 %all-to-all-start.7 = ((bf16[4,1,64,16,512]{4,3,2,1,0:T(8,128)(2,1)}), bf16[4,1,64,16,512]{4,3,2,1,0:T(8,128)(2,1)}, u32[]{:S(2)}, u32[]{:S(2)}) async-start(bf16[4,1,64,16,512]{4,3,2,1,0:T(8,128)(2,1)} %bitcast.209), calls=%async_computation.7 | async-start | bytes 8388608 | tf_op jit(solution)/shard_map/all_to_all | solution.py:47
  795.7 146.1 %reduce-scatter.8.cloned.1.call-start = ((), (), s32[]{:S(2)}) async-start(), calls=%async_computation.18 | async-start | bytes 2621440 | tf_op jit(solution)/shard_map/reduce_scatter | solution.py:21
  888.4 11.5 %copy-start.6 = (bf16[64,4,1,16,256]{4,3,2,1,0:T(8,128)(2,1)S(1)}, bf16[64,4,1,16,256]{4,3,2,1,0:T(8,128)(2,1)}, u32[]{:S(2)}) copy-start(bf16[64,4,1,16,256]{4,3,2,1,0:T(8,128)(2,1)} %get-tuple-element.58) | copy-start | bytes 6291460
  919.2 22.6 %copy-start.7 = (bf16[64,48,256]{2,1,0:T(8,128)(2,1)S(1)}, bf16[64,48,256]{2,1,0:T(8,128)(2,1)}, u32[]{:S(2)}) copy-start(bf16[64,48,256]{2,1,0:T(8,128)(2,1)} %reduce-scatter.4.cloned.1.call-done) | copy-start | bytes 4718596
Sparse Core Ops, SparseCore 0:
  10.2 25.2 all-gather.9
  49.8 23.0 all-gather.7
  74.4 22.5 all-gather.11
  147.8 23.0 all-gather.13
  172.8 58.2 all-gather.5
  569.4 72.1 reduce-scatter.5
  790.8 56.5 reduce-scatter.3
  900.0 29.5 reduce-scatter.7
where the time goes:
time: 960 us; the launch traced here: 952 us
  waiting for transfers between devices  456 us (48%)
  matrix products  250 us (26%)
  local copies, waits for them, and re-layouts  101 us (11%)
  other arithmetic  88.4 us (9%)
  starting transfers between devices  40.7 us (4%)
  between operations  14.9 us (2%)
    all_to_all x8, waiting for transfers between devices, exchange(): return lax.all_to_all(part, 'seq', split_axis=0, concat_axis=0, tiled=True)  404 us
    dot_general x4, matrix products, through_first(): jnp.einsum('istk,sbitc->bikc', first_split[:, :, q], back, preferred_elem...  98.4 us
    dot_general x1, matrix products, shards(): jnp.einsum('jik,bkjc->bjic', second_full, exchanged, preferred_element_ty...  51.6 us
    all_gather x4, waiting for transfers between devices, shards(): factor = lax.all_gather(first_factor[own], 'dp', axis=1, tiled=True)  50 us
    dot_general x4, matrix products, through_first(): jnp.einsum('sbitc,bikc->istk', back, blocked, preferred_element_type=f32)  43.1 us
    mul x1, other arithmetic, shards(): total = (cot_f32 * mixing * gate_slope).reshape(blocked.shape)  40.1 us
    all_to_all x8, starting transfers between devices, exchange(): return lax.all_to_all(part, 'seq', split_axis=0, concat_axis=0, tiled=True)  40 us
    optimization_barrier x1, local copies, waits for them, and re-layouts, after(): kept = lax.optimization_barrier((value,) + others)  33.7 us
  transfers between devices with their start and end apart: 16, of which 9 were waited for; matrix products, arithmetic and copies ran while one was open for 43% of the time, Pallas kernels for 0%

commit v1 on v0

--- a/solution.py
+++ b/solution.py
@@ -4,6 +4,18 @@
 from jax import lax
 from jax.experimental.layout import Layout, with_layout_constraint
 from jax.sharding import PartitionSpec as P
+
+
+def collect(array, axis, dim):
+    ways, here, turn = (lax.axis_size(axis), lax.axis_index(axis), array.shape[dim])
+    line, have = (array, 1)
+    while have < ways:
+        line = jnp.concatenate(
+            [line, lax.ppermute(line, axis, [(d, (d - have) % ways) for d in range(ways)])],
+            axis=dim,
+        )
+        have = 2 * have
+    return jnp.roll(line, here * turn, axis=dim)
 
 
 def silu_parts(values):
@@ -49,7 +61,7 @@
     first_parts, received = ([], [])
     for q in range(chunks):
         own = slice(q * ic, (q + 1) * ic)
-        factor = lax.all_gather(first_factor[own], "dp", axis=1, tiled=True)
+        factor = collect(first_factor[own], "dp", 1)
         first_parts.append(factor)
         part = jnp.einsum(
             "ijk,bikc->bijc", factor, blocked[:, own], preferred_element_type=f32

time: 960 us -> 974 us (1.015)
  waiting for transfers between devices: 456 us -> 437 us
  starting transfers between devices: 40.7 us -> 57.8 us
  other arithmetic: 88.4 us -> 103 us
    ppermute x0 -> x8, waiting for transfers between devices: none -> 132 us  [collect(): lax.ppermute(line, axis, [(d, (d - have) % ways) for d in range(ways)])]
    all_to_all x8, waiting for transfers between devices: 404 us -> 306 us  [exchange(): return lax.all_to_all(part, 'seq', split_axis=0, concat_axis=0, tiled=True)]
    all_gather x4 -> x0, waiting for transfers between devices: 50 us -> none  [shards(): factor = lax.all_gather(first_factor[own], 'dp', axis=1, tiled=True)]
    ppermute x0 -> x8, starting transfers between devices: none -> 17.4 us  [collect(): lax.ppermute(line, axis, [(d, (d - have) % ways) for d in range(ways)])]
    concatenate x0 -> x8, other arithmetic: none -> 14.4 us  [the longest x4 12.2 us: collect(): return jnp.roll(line, here * turn, axis=dim)]
  transfers between devices with their start and end apart: 16 -> 20, of which waited for: 9 -> 15; matrix products, arithmetic and copies ran while one was open for 43% -> 44% of each run, Pallas kernels for 0% -> 0%
where the time goes in v1:
time: 974 us; the launch traced here: 963 us
  waiting for transfers between devices  437 us (45%)
  matrix products  250 us (26%)
  other arithmetic  103 us (11%)
  local copies, waits for them, and re-layouts  100 us (10%)
  starting transfers between devices  57.8 us (6%)
  between operations  14.6 us (1%)
    all_to_all x8, waiting for transfers between devices, exchange(): return lax.all_to_all(part, 'seq', split_axis=0, concat_axis=0, tiled=True)  306 us
    ppermute x8, waiting for transfers between devices, collect(): lax.ppermute(line, axis, [(d, (d - have) % ways) for d in range(ways)])  132 us
    dot_general x4, matrix products, through_first(): jnp.einsum('istk,sbitc->bikc', first_split[:, :, q], back, preferred_elem...  98.2 us
    dot_general x1, matrix products, shards(): jnp.einsum('jik,bkjc->bjic', second_full, exchanged, preferred_element_ty...  51.6 us
    dot_general x4, matrix products, through_first(): jnp.einsum('sbitc,bikc->istk', back, blocked, preferred_element_type=f32)  43.1 us
    mul x1, other arithmetic, shards(): total = (cot_f32 * mixing * gate_slope).reshape(blocked.shape)  40.1 us
    all_to_all x8, starting transfers between devices, exchange(): return lax.all_to_all(part, 'seq', split_axis=0, concat_axis=0, tiled=True)  39.8 us
    optimization_barrier x1, local copies, waits for them, and re-layouts, after(): kept = lax.optimization_barrier((value,) + others)  33.7 us
  transfers between devices with their start and end apart: 20, of which 15 were waited for; matrix products, arithmetic and copies ran while one was open for 44% of the time, Pallas kernels for 0%

profile of v1, /device:TPU:0, one launch (start us, length us, event | category | flops | bytes accessed | tf_op | source)
XLA Modules:
  0.0 963.3 jit_solution(9260758141317014369)
XLA Ops:
  19.6 25.7 %collective-permute-done.3 = bf16[16,128,256]{2,1,0:T(8,128)(2,1)} collective-permute-done((bf16[16,128,256]{2,1,0:T(8,128)(2,1)}, bf16[16,128,256]{2,1,0:T(8,128)(2,1)}, u32[]{:S(2)}, u32[]{:S(2)}) %collective-permute-start.3) | collective-permute-done | bytes 1048608 | tf_op jit(solution)/shard_map/ppermute | solution.py:14
  68.3 23.3 %collective-permute-done.1 = bf16[16,128,256]{2,1,0:T(8,128)(2,1)S(1)} collective-permute-done((bf16[16,128,256]{2,1,0:T(8,128)(2,1)S(1)}, bf16[16,128,256]{2,1,0:T(8,128)(2,1)S(1)}, u32[]{:S(2)}, u32[]{:S(2)}) %collective-permute-start.1) | collective-permute-done | bytes 1048608 | tf_op jit(solution)/shard_map/ppermute | solution.py:14
  101.0 52.4 %all-to-all-done = bf16[4,1,16,64,512]{4,3,2,1,0:T(8,128)(2,1)} async-done(((bf16[4,1,16,64,512]{4,3,2,1,0:T(8,128)(2,1)}), bf16[4,1,16,64,512]{4,3,2,1,0:T(8,128)(2,1)}, u32[]{:S(2)}, u32[]{:S(2)}) %all-to-all-start) | async-done | bytes 4194336 | tf_op jit(solution)/shard_map/all_to_all | solution.py:59
  170.3 31.9 %collective-permute-done.5 = bf16[16,128,256]{2,1,0:T(8,128)(2,1)} collective-permute-done((bf16[16,128,256]{2,1,0:T(8,128)(2,1)}, bf16[16,128,256]{2,1,0:T(8,128)(2,1)}, u32[]{:S(2)}, u32[]{:S(2)}) %collective-permute-start.5) | collective-permute-done | bytes 1048608 | tf_op jit(solution)/shard_map/ppermute | solution.py:14
  211.9 39.2 %all-to-all-done.1 = bf16[4,1,16,64,512]{4,3,2,1,0:T(8,128)(2,1)} async-done(((bf16[4,1,16,64,512]{4,3,2,1,0:T(8,128)(2,1)}), bf16[4,1,16,64,512]{4,3,2,1,0:T(8,128)(2,1)}, u32[]{:S(2)}, u32[]{:S(2)}) %all-to-all-start.1) | async-done | bytes 4194336 | tf_op jit(solution)/shard_map/all_to_all | solution.py:59
  274.7 23.9 %collective-permute-done.7 = bf16[16,128,256]{2,1,0:T(8,128)(2,1)S(1)} collective-permute-done((bf16[16,128,256]{2,1,0:T(8,128)(2,1)S(1)}, bf16[16,128,256]{2,1,0:T(8,128)(2,1)S(1)}, u32[]{:S(2)}, u32[]{:S(2)}) %collective-permute-start.7) | collective-permute-done | bytes 1048608 | tf_op jit(solution)/shard_map/ppermute | solution.py:14
  308.0 40.6 %all-to-all-done.2 = bf16[4,1,16,64,512]{4,3,2,1,0:T(8,128)(2,1)} async-done(((bf16[4,1,16,64,512]{4,3,2,1,0:T(8,128)(2,1)}), bf16[4,1,16,64,512]{4,3,2,1,0:T(8,128)(2,1)}, u32[]{:S(2)}, u32[]{:S(2)}) %all-to-all-start.2) | async-done | bytes 4194336 | tf_op jit(solution)/shard_map/all_to_all | solution.py:59
  353.5 21.3 %fusion = bf16[1,16384,512]{2,1,0:T(8,128)(2,1)} fusion(bf16[1,16384,512]{2,1,0:T(8,128)(2,1)} %param.7, bf16[1,16384,512]{2,1,0:T(8,128)(2,1)} %param.6), kind=kLoop, calls=%fused_computation.5 | loop fusion | flops 67108864 | bytes 50331648 | tf_op jit(solution)/shard_map/convert_element_type | solution.py:75
  400.1 46.1 %all-to-all-done.3 = bf16[4,1,16,64,512]{4,3,2,1,0:T(8,128)(2,1)} async-done(((bf16[4,1,16,64,512]{4,3,2,1,0:T(8,128)(2,1)}), bf16[4,1,16,64,512]{4,3,2,1,0:T(8,128)(2,1)}, u32[]{:S(2)}, u32[]{:S(2)}) %all-to-all-start.3) | async-done | bytes 4194336 | tf_op jit(solution)/shard_map/all_to_all | solution.py:59
  451.5 14.0 %pad_maximum_fusion = bf16[4,1,64,64,512]{4,3,2,1,0:T(8,128)(2,1)} fusion(bf16[4,1,16,64,512]{4,3,2,1,0:T(8,128)(2,1)} %all-to-all-done.3, bf16[4,1,16,64,512]{4,3,2,1,0:T(8,128)(2,1)} %all-to-all-done.2, bf16[4,1,16,64,512]{4,3,2,1,0:T(8,128)(2,1)} %all-to-all-done.1, bf16[4,1,16,64,512]{4,3,2,1,0:T(8,128)(2,1)} %all-to-all-done), kind=kLoop, calls=%fused_computation.19 | loop fusion | flops 25165824 | bytes 33554432 | tf_op jit(solution)/shard_map/concatenate | solution.py:101
  465.5 51.6 %fusion.11 = f32[64,512,256]{1,2,0:T(8,128)} fusion(bf16[256,64,512]{2,1,0:T(8,128)(2,1)} %bitcast.205, bf16[64,256,256]{2,0,1:T(8,128)(2,1)} %all-gather.2.cloned.1.call-done), kind=kOutput, calls=%fused_computation.23 | convolution fusion | flops 4294967296 | bytes 58720256 | tf_op jit(solution)/shard_map/jik,bkjc->bjic/dot_general | solution.py:103
  517.1 40.1 %fusion.1 = (f32[1,16384,512]{2,1,0:T(8,128)}, bf16[1,16384,512]{2,1,0:T(8,128)(2,1)}) fusion(bf16[1,16384,512]{2,1,0:T(8,128)(2,1)} %param.7, bf16[1,16384,512]{2,1,0:T(8,128)(2,1)} %param.6, f32[64,512,256]{1,2,0:T(8,128)} %fusion.11), kind=kLoop, calls=%fused_computation.6 | loop fusion | flops 117440512 | bytes 117440512 | tf_op jit(solution)/shard_map/mul | solution.py:111
  557.2 24.3 %multiply_convert_fusion = bf16[64,256,256]{2,1,0:T(8,128)(2,1)} fusion(bf16[64,256,512]{2,1,0:T(8,128)(2,1)} %bitcast.207, bf16[256,64,512]{2,1,0:T(8,128)(2,1)} %bitcast.206), kind=kOutput, calls=%fused_computation.20 | convolution fusion | flops 4303355904 | bytes 41943040 | tf_op jit(solution)/shard_map/bjic,bkjc->jik/dot_general | solution.py:107
  612.4 33.7 %copy.73 = f32[1,64,256,512]{2,3,1,0:T(8,128)} copy(f32[1,64,256,512]{3,2,1,0:T(8,128)} %bitcast.204) | data formatting | bytes 67108864 | tf_op jit(solution)/shard_map/optimization_barrier | solution.py:55
  646.1 17.9 %fusion.56 = f32[64,512,256,1]{2,1,0,3:T(8,128)} fusion(bf16[64,4,1,16,256]{4,3,2,1,0:T(8,128)(2,1)S(1)} %get-tuple-element.62, bf16[4,1,64,16,512]{4,3,2,1,0:T(8,128)(2,1)} %all-to-all-done.4), kind=kOutput, calls=%fused_computation.117 | convolution fusion | flops 1073741824 | bytes 39845888 | tf_op jit(solution)/shard_map/istk,sbitc->bikc/dot_general | solution.py:86
  664.0 24.8 %all-to-all-done.5 = bf16[4,1,64,16,512]{4,3,2,1,0:T(8,128)(2,1)} async-done(((bf16[4,1,64,16,512]{4,3,2,1,0:T(8,128)(2,1)}), bf16[4,1,64,16,512]{4,3,2,1,0:T(8,128)(2,1)}, u32[]{:S(2)}, u32[]{:S(2)}) %all-to-all-start.5) | async-done | bytes 4194336 | tf_op jit(solution)/shard_map/all_to_all | solution.py:59
  704.0 11.3 %multiply_convert_fusion.3 = bf16[64,4,16,256]{3,2,1,0:T(8,128)(2,1)} fusion(bf16[64,256,512,1]{2,1,3,0:T(8,128)(2,1)} %bitcast.201, bf16[4,1,64,16,512]{4,3,2,1,0:T(8,128)(2,1)} %all-to-all-done.5), kind=kOutput, calls=%fused_computation.82 | convolution fusion | flops 1075838976 | bytes 23068672 | tf_op jit(solution)/shard_map/sbitc,bikc->istk/dot_general | solution.py:83
  715.2 35.8 %bitcast_add_fusion.2 = f32[1,64,256,512]{2,3,1,0:T(8,128)} fusion(f32[1,64,256,512]{2,3,1,0:T(8,128)} %copy.73, f32[64,512,256,1]{2,1,0,3:T(8,128)} %fusion.56, bf16[64,4,1,16,256]{4,3,2,1,0:T(8,128)(2,1)} %get-tuple-element.61, bf16[4,1,64,16,512]{4,3,2,1,0:T(8,128)(2,1)} %all-to-all-done.5), kind=kOutput, calls=%fused_computation.15 | convolution fusion | flops 1090519040 | bytes 106954752 | tf_op jit(solution)/shard_map/istk,sbitc->bikc/dot_general | solution.py:86
  751.1 35.3 %all-to-all-done.6 = bf16[4,1,64,16,512]{4,3,2,1,0:T(8,128)(2,1)} async-done(((bf16[4,1,64,16,512]{4,3,2,1,0:T(8,128)(2,1)}), bf16[4,1,64,16,512]{4,3,2,1,0:T(8,128)(2,1)}, u32[]{:S(2)}, u32[]{:S(2)}) %all-to-all-start.6) | async-done | bytes 4194336 | tf_op jit(solution)/shard_map/all_to_all | solution.py:59
  807.9 25.4 %bitcast_add_fusion.1 = f32[1,64,256,512]{2,3,1,0:T(8,128)} fusion(f32[1,64,256,512]{2,3,1,0:T(8,128)} %bitcast_add_fusion.2, bf16[64,4,1,16,256]{4,3,2,1,0:T(8,128)(2,1)S(1)} %copy-done.7, bf16[4,1,64,16,512]{4,3,2,1,0:T(8,128)(2,1)} %all-to-all-done.6), kind=kOutput, calls=%fused_computation.14 | convolution fusion | flops 1082130432 | bytes 73400320 | tf_op jit(solution)/shard_map/istk,sbitc->bikc/dot_general | solution.py:86
  833.3 67.2 %all-to-all-done.7 = bf16[4,1,64,16,512]{4,3,2,1,0:T(8,128)(2,1)} async-done(((bf16[4,1,64,16,512]{4,3,2,1,0:T(8,128)(2,1)}), bf16[4,1,64,16,512]{4,3,2,1,0:T(8,128)(2,1)}, u32[]{:S(2)}, u32[]{:S(2)}) %all-to-all-start.7) | async-done | bytes 4194336 | tf_op jit(solution)/shard_map/all_to_all | solution.py:59
  900.5 11.5 %multiply_convert_fusion.1 = bf16[64,4,16,256]{3,2,1,0:T(8,128)(2,1)} fusion(bf16[64,256,512,1]{2,1,3,0:T(8,128)(2,1)} %bitcast.203, bf16[4,1,64,16,512]{4,3,2,1,0:T(8,128)(2,1)} %all-to-all-done.7), kind=kOutput, calls=%fused_computation.80 | convolution fusion | flops 1075838976 | bytes 23068672 | tf_op jit(solution)/shard_map/sbitc,bikc->istk/dot_general | solution.py:83
  912.0 19.0 %fusion.7 = bf16[1,64,256,512]{2,3,1,0:T(8,128)(2,1)} fusion(f32[1,64,256,512]{2,3,1,0:T(8,128)} %bitcast_add_fusion.1, bf16[64,4,1,16,256]{4,3,2,1,0:T(8,128)(2,1)S(1)} %copy-done.11, bf16[4,1,64,16,512]{4,3,2,1,0:T(8,128)(2,1)} %all-to-all-done.7), kind=kOutput, calls=%fused_computation.13 | convolution fusion | flops 1090519040 | bytes 56623104 | tf_op jit(solution)/shard_map/istk,sbitc->bikc/dot_general | solution.py:86
  931.0 22.6 %copy.81 = bf16[1,64,256,512]{3,2,1,0:T(8,128)(2,1)} copy(bf16[1,64,256,512]{2,3,1,0:T(8,128)(2,1)} %fusion.7) | data formatting | bytes 33554432 | tf_op jit(solution)/shard_map/convert_element_type | solution.py:139
  (92 shorter events, 209.9 us)
Async XLA Ops:
  8.8 9.1 collective-permute-start.2
  19.0 26.2 %collective-permute-start.3 = (bf16[16,128,256]{2,1,0:T(8,128)(2,1)}, bf16[16,128,256]{2,1,0:T(8,128)(2,1)}, u32[]{:S(2)}, u32[]{:S(2)}) collective-permute-start(bf16[16,128,256]{2,1,0:T(8,128)(2,1)} %pad_maximum_fusion.4), channel_id=1, source_target_pairs={{0,2},{1,3},{2,0},{3,1},{4,6},{5,7},{6,4},{7,5},{8,10},{9,11},{10,... | collective-permute-start | bytes 3145736 | tf_op jit(solution)/shard_map/ppermute | solution.py:14
  54.9 98.5 %all-to-all-start = ((bf16[4,1,16,64,512]{4,3,2,1,0:T(8,128)(2,1)}), bf16[4,1,16,64,512]{4,3,2,1,0:T(8,128)(2,1)}, u32[]{:S(2)}, u32[]{:S(2)}) async-start(bf16[4,1,16,64,512]{4,3,2,1,0:T(8,128)(2,1)} %bitcast.222), calls=%async_computation | async-start | bytes 8388608 | tf_op jit(solution)/shard_map/all_to_all | solution.py:59
  59.8 6.9 collective-permute-start
  66.7 24.9 %collective-permute-start.1 = (bf16[16,128,256]{2,1,0:T(8,128)(2,1)S(1)}, bf16[16,128,256]{2,1,0:T(8,128)(2,1)S(1)}, u32[]{:S(2)}, u32[]{:S(2)}) collective-permute-start(bf16[16,128,256]{2,1,0:T(8,128)(2,1)S(1)} %pad_maximum_fusion.3), channel_id=1, source_target_pairs={{0,2},{1,3},{2,0},{3,1},{4,6},{5,7},{6,4},{7,5},{8,10},{9,11},{10,... | collective-permute-start | bytes 3145736 | tf_op jit(solution)/shard_map/ppermute | solution.py:14
  153.4 14.4 %copy-start.9 = (bf16[64,64,256]{2,1,0:T(8,128)(2,1)S(1)}, bf16[64,64,256]{2,1,0:T(8,128)(2,1)}, u32[]{:S(2)}) copy-start(bf16[64,64,256]{2,1,0:T(8,128)(2,1)} %param.9) | copy-start | bytes 6291460
  153.4 97.7 %all-to-all-start.1 = ((bf16[4,1,16,64,512]{4,3,2,1,0:T(8,128)(2,1)}), bf16[4,1,16,64,512]{4,3,2,1,0:T(8,128)(2,1)}, u32[]{:S(2)}, u32[]{:S(2)}) async-start(bf16[4,1,16,64,512]{4,3,2,1,0:T(8,128)(2,1)} %bitcast.218), calls=%async_computation.1 | async-start | bytes 8388608 | tf_op jit(solution)/shard_map/all_to_all | solution.py:59
  158.4 216.4 %all-gather.2.cloned.1.call-start = ((), (), s32[]{:S(2)}) async-start(), calls=%async_computation.11 | async-start | bytes 10485760 | tf_op jit(solution)/shard_map/all_gather | solution.py:74
  158.5 6.8 collective-permute-start.4
  167.1 35.1 %collective-permute-start.5 = (bf16[16,128,256]{2,1,0:T(8,128)(2,1)}, bf16[16,128,256]{2,1,0:T(8,128)(2,1)}, u32[]{:S(2)}, u32[]{:S(2)}) collective-permute-start(bf16[16,128,256]{2,1,0:T(8,128)(2,1)} %pad_maximum_fusion.5), channel_id=1, source_target_pairs={{0,2},{1,3},{2,0},{3,1},{4,6},{5,7},{6,4},{7,5},{8,10},{9,11},{10,... | collective-permute-start | bytes 3145736 | tf_op jit(solution)/shard_map/ppermute | solution.py:14
  251.1 97.5 %all-to-all-start.2 = ((bf16[4,1,16,64,512]{4,3,2,1,0:T(8,128)(2,1)}), bf16[4,1,16,64,512]{4,3,2,1,0:T(8,128)(2,1)}, u32[]{:S(2)}, u32[]{:S(2)}) async-start(bf16[4,1,16,64,512]{4,3,2,1,0:T(8,128)(2,1)} %bitcast.220), calls=%async_computation.2 | async-start | bytes 8388608 | tf_op jit(solution)/shard_map/all_to_all | solution.py:59
  256.0 17.4 %collective-permute-start.6 = (bf16[16,64,256]{2,1,0:T(8,128)(2,1)S(1)}, bf16[16,64,256]{2,1,0:T(8,128)(2,1)S(1)}, u32[]{:S(2)}, u32[]{:S(2)}) collective-permute-start(bf16[16,64,256]{2,1,0:T(8,128)(2,1)S(1)} %get-tuple-element.69), channel_id=1, source_target_pairs={{0,3},{1,0},{2,1},{3,2},{4,7},{5,4},{6,5},{7,6},{8,11},{9,8},{10,9... | collective-permute-start | bytes 1572872 | tf_op jit(solution)/shard_map/ppermute | solution.py:14
  273.4 25.2 %collective-permute-start.7 = (bf16[16,128,256]{2,1,0:T(8,128)(2,1)S(1)}, bf16[16,128,256]{2,1,0:T(8,128)(2,1)S(1)}, u32[]{:S(2)}, u32[]{:S(2)}) collective-permute-start(bf16[16,128,256]{2,1,0:T(8,128)(2,1)S(1)} %pad_maximum_fusion.6), channel_id=1, source_target_pairs={{0,2},{1,3},{2,0},{3,1},{4,6},{5,7},{6,4},{7,5},{8,10},{9,11},{10,... | collective-permute-start | bytes 3145736 | tf_op jit(solution)/shard_map/ppermute | solution.py:14
  348.7 97.5 %all-to-all-start.3 = ((bf16[4,1,16,64,512]{4,3,2,1,0:T(8,128)(2,1)}), bf16[4,1,16,64,512]{4,3,2,1,0:T(8,128)(2,1)}, u32[]{:S(2)}, u32[]{:S(2)}) async-start(bf16[4,1,16,64,512]{4,3,2,1,0:T(8,128)(2,1)} %bitcast.223), calls=%async_computation.3 | async-start | bytes 8388608 | tf_op jit(solution)/shard_map/all_to_all | solution.py:59
  446.2 144.4 %all-to-all-start.4 = ((bf16[4,1,64,16,512]{4,3,2,1,0:T(8,128)(2,1)}), bf16[4,1,64,16,512]{4,3,2,1,0:T(8,128)(2,1)}, u32[]{:S(2)}, u32[]{:S(2)}) async-start(bf16[4,1,64,16,512]{4,3,2,1,0:T(8,128)(2,1)} %bitcast.219), calls=%async_computation.4 | async-start | bytes 8388608 | tf_op jit(solution)/shard_map/all_to_all | solution.py:59
  451.1 382.2 %reduce-scatter.6.cloned.1.call-start = ((), (), s32[]{:S(2)}) async-start(), calls=%async_computation.13 | async-start | bytes 10485760 | tf_op jit(solution)/shard_map/reduce_scatter | solution.py:113
  590.6 98.2 %all-to-all-start.5 = ((bf16[4,1,64,16,512]{4,3,2,1,0:T(8,128)(2,1)}), bf16[4,1,64,16,512]{4,3,2,1,0:T(8,128)(2,1)}, u32[]{:S(2)}, u32[]{:S(2)}) async-start(bf16[4,1,64,16,512]{4,3,2,1,0:T(8,128)(2,1)} %bitcast.221), calls=%async_computation.5 | async-start | bytes 8388608 | tf_op jit(solution)/shard_map/all_to_all | solution.py:59
  688.8 97.5 %all-to-all-start.6 = ((bf16[4,1,64,16,512]{4,3,2,1,0:T(8,128)(2,1)}), bf16[4,1,64,16,512]{4,3,2,1,0:T(8,128)(2,1)}, u32[]{:S(2)}, u32[]{:S(2)}) async-start(bf16[4,1,64,16,512]{4,3,2,1,0:T(8,128)(2,1)} %bitcast.216), calls=%async_computation.6 | async-start | bytes 8388608 | tf_op jit(solution)/shard_map/all_to_all | solution.py:59
  693.7 206.8 %reduce-scatter.4.cloned.1.call-start = ((), (), s32[]{:S(2)}) async-start(), calls=%async_computation.12 | async-start | bytes 7864320 | tf_op jit(solution)/shard_map/reduce_scatter | solution.py:33
  786.4 10.1 %copy-start.6 = (bf16[64,4,16,256]{3,2,1,0:T(8,128)(2,1)S(1)}, bf16[64,4,16,256]{3,2,1,0:T(8,128)(2,1)}, u32[]{:S(2)}) copy-start(bf16[64,4,16,256]{3,2,1,0:T(8,128)(2,1)} %multiply_convert_fusion.3) | copy-start | bytes 6291460
  802.8 97.7 %all-to-all-start.7 = ((bf16[4,1,64,16,512]{4,3,2,1,0:T(8,128)(2,1)}), bf16[4,1,64,16,512]{4,3,2,1,0:T(8,128)(2,1)}, u32[]{:S(2)}, u32[]{:S(2)}) async-start(bf16[4,1,64,16,512]{4,3,2,1,0:T(8,128)(2,1)} %bitcast.217), calls=%async_computation.7 | async-start | bytes 8388608 | tf_op jit(solution)/shard_map/all_to_all | solution.py:59
  807.8 145.8 %reduce-scatter.8.cloned.1.call-start = ((), (), s32[]{:S(2)}) async-start(), calls=%async_computation.14 | async-start | bytes 2621440 | tf_op jit(solution)/shard_map/reduce_scatter | solution.py:33
  900.5 11.5 %copy-start.11 = (bf16[64,4,1,16,256]{4,3,2,1,0:T(8,128)(2,1)S(1)}, bf16[64,4,1,16,256]{4,3,2,1,0:T(8,128)(2,1)}, u32[]{:S(2)}) copy-start(bf16[64,4,1,16,256]{4,3,2,1,0:T(8,128)(2,1)} %get-tuple-element.59) | copy-start | bytes 6291460
  931.0 22.6 %copy-start.12 = (bf16[64,48,256]{2,1,0:T(8,128)(2,1)S(1)}, bf16[64,48,256]{2,1,0:T(8,128)(2,1)}, u32[]{:S(2)}) copy-start(bf16[64,48,256]{2,1,0:T(8,128)(2,1)} %reduce-scatter.4.cloned.1.call-done) | copy-start | bytes 4718596
  (9 other events, 41.0 us)
Sparse Core Ops, SparseCore 0:
  170.4 69.5 all-gather.1
  581.6 72.8 reduce-scatter.5
  802.9 57.2 reduce-scatter.3
  912.1 30.3 reduce-scatter.7
